TPU v7x, 256 devices: a whole 4x4x8 slice. The times are simulated.
256 devices in a mesh: dp: 8 (over y, core), rows: 32 (over z, x).
Axes of the slice: x: 4, y: 4, z: 8, core: 2. Of those that a mesh axis runs over, the one named last changes fastest.
Arguments:
- grads: bfloat16 [8, 4, 1024, 8192], P('dp', None, 'rows'), may hold values from -120 to 120
- errors: float32 [8, 4, 1024, 8192], P('dp', None, 'rows'), may hold values from -3 to 3
- q_prev: float32 [4, 8192, 64], P(None, 'rows'), may hold values from -0.0625 to 0.0625
Outputs:
- q_new: float32 [4, 8192, 64], P(None, 'rows')
- errors_new: float32 [8, 4, 1024, 8192], P('dp', None, 'rows')
All inputs are finite; a program needn't handle non-finite values.
Results may differ from a plain program's by a relative error of at most 0.0003.
Values sent between devices are 32-bit elements; how exact they have to be, the bound alone decides.
A program may use at most 128 MiB of HBM per device.

v0:
```python
import jax
import jax.numpy as jnp
from jax import lax
from jax.sharding import PartitionSpec as P


def orthonormal(left, gram):
    trace = jnp.trace(gram, axis1=1, axis2=2)
    eye = jnp.eye(gram.shape[1], dtype=gram.dtype)
    factor = jnp.linalg.cholesky(gram + (0.0001 * trace / gram.shape[1])[:, None, None] * eye[None])
    solved = jax.vmap(lambda low, rhs: jax.scipy.linalg.solve_triangular(low, rhs, lower=True))(
        factor, jnp.transpose(left, (0, 2, 1))
    )
    return jnp.transpose(solved, (0, 2, 1))


def body(grads, errors, q_prev):
    merged = grads[0].astype(jnp.float32) + errors[0]
    groups = lax.axis_size("dp")
    width = merged.shape[2]
    partial_left = jnp.einsum(
        "mrc,mck->mrk",
        merged,
        lax.all_gather(q_prev, "rows", axis=1, tiled=True),
        precision=lax.Precision.HIGHEST,
    )
    left = lax.psum(partial_left, "dp") / groups
    local_gram = jnp.einsum("mrk,mrl->mkl", left, left, precision=lax.Precision.HIGHEST)
    gram = lax.psum(local_gram, "rows")
    ortho = orthonormal(left, gram)
    term = jnp.einsum("mrc,mrk->mck", merged, ortho, precision=lax.Precision.HIGHEST)
    q_all = lax.psum(term, ("dp", "rows")) / groups
    share = width // lax.axis_size("rows")
    q_mine = lax.dynamic_slice_in_dim(q_all, lax.axis_index("rows") * share, share, 1)
    approx = jnp.einsum("mrk,mck->mrc", ortho, q_all, precision=lax.Precision.HIGHEST)
    errors_new = merged - approx
    return (q_mine, errors_new[None])


def solution(mesh):
    return jax.shard_map(
        body,
        mesh=mesh,
        in_specs=(P("dp", None, "rows", None), P("dp", None, "rows", None), P(None, "rows", None)),
        out_specs=(P(None, "rows", None), P("dp", None, "rows", None)),
        check_vma=False,
    )
```

profile of v0, /device:TPU:1, one launch (start us, length us, event | category | flops | bytes accessed | tf_op | source)
XLA Modules:
  0.0 646.3 jit_solution(5171255512652250015)
XLA Ops:
  7.2 0.0 all-gather.2.cloned.1.call-start
  7.2 0.7 all-gather.2.cloned.1.call-update
  7.9 0.0 all-reduce.3.cloned.1.call-start
  8.0 107.5 %all-gather.2.cloned.1.call-done = f32[4,8192,64]{1,2,0:T(8,128)} async-done(((f32[4,256,64]{1,2,0:T(8,128)}), f32[4,8192,64]{1,2,0:T(8,128)}) %all-gather.2.cloned.1.call-update) | async-done | bytes 8388624 | tf_op jit(solution)/shard_map/all_gather | solution.py:24
  115.5 10.5 %fusion.3 = f32[4,32,64]{2,1,0:T(8,128)S(1)} fusion(f32[4,8192,64]{1,2,0:T(8,128)} %all-gather.2.cloned.1.call-done, f32[1,4,32,8192]{3,2,1,0:T(8,128)} %param.4, bf16[1,4,32,8192]{3,2,1,0:T(8,128)(2,1)} %param.3), kind=kOutput, calls=%fused_computation.4 | convolution fusion | flops 807403520 | bytes 14712832 | tf_op jit(solution)/shard_map/mrc,mck->mrk/dot_general | solution.py:21
  126.0 23.9 %psum.21 = f32[4,32,64]{2,1,0:T(8,128)S(1)} all-reduce(f32[4,32,64]{2,1,0:T(8,128)S(1)} %fusion.3), channel_id=1, replica_groups=mesh['dp'=8,'rows'=32] {'dp'}, use_global_device_ids=true, to_apply=%region_0.0 | all-reduce | flops 8192 | bytes 65536 | tf_op jit(solution)/shard_map/psum | solution.py:27
  149.9 1.1 fusion.9
  150.9 0.0 all-reduce.3.cloned.1.call-update
  150.9 0.2 all-reduce.5.cloned.1.call-start
  151.2 134.8 %all-reduce.3.cloned.1.call-done = f32[4,64,64]{2,1,0:T(8,128)} async-done(((f32[4,64,64]{2,1,0:T(8,128)}), f32[4,64,64]{2,1,0:T(8,128)}) %all-reduce.3.cloned.1.call-update) | async-done | bytes 65552 | tf_op jit(solution)/shard_map/psum | solution.py:29
  286.0 1.0 select_reduce_fusion.1
  287.1 1.0 multiply_add_fusion
  288.0 0.1 copy.7
  288.1 1.0 fusion.7
  289.1 23.5 %custom-call.8 = f32[4,64,64]{2,1,0:T(8,128)S(1)} custom-call(f32[4,64,64]{2,1,0:T(8,128)S(1)} %fusion.7), custom_call_target="Cholesky" | custom-call | tf_op jit(solution)/shard_map/jit(cholesky)/cholesky | solution.py:10
  312.6 0.1 compare_reduce_fusion
  312.8 0.1 select_bitcast_fusion
  312.9 19.7 %custom-call.9 = f32[4,1,64,64]{2,3,1,0:T(8,128)S(1)} custom-call(f32[4,1,64,64]{3,2,1,0:T(8,128)S(1)} %select_bitcast_fusion), custom_call_target="InvertDiagBlocksLowerTriangular" | custom-call | tf_op jit(solution)/shard_map/vmap(jit(_solve_triangular))/triangular_solve | solution.py:11
  332.5 0.3 fusion.5
  332.8 10.6 %fusion.1 = f32[4,8192,64]{1,2,0:T(8,128)} fusion(f32[4,64,32]{1,2,0:T(8,128)S(1)} %fusion.5, f32[1,4,32,8192]{3,2,1,0:T(8,128)} %param.4, bf16[1,4,32,8192]{3,2,1,0:T(8,128)(2,1)S(1)} %copy-done.2), kind=kOutput, calls=%fused_computation.2 | convolution fusion | flops 807403520 | bytes 14712832 | tf_op jit(solution)/shard_map/mrc,mrk->mck/dot_general | solution.py:31
  343.4 279.5 %all-reduce.5.cloned.1.call-done = f32[4,8192,64]{1,2,0:T(8,128)} async-done(((f32[4,8192,64]{1,2,0:T(8,128)}), f32[4,8192,64]{1,2,0:T(8,128)}) %all-reduce.5.cloned.1.call-update) | async-done | bytes 8388624 | tf_op jit(solution)/shard_map/psum | solution.py:32
  622.9 8.7 %broadcast_multiply_fusion = f32[4,8192,64]{1,2,0:T(8,128)} fusion(f32[4,8192,64]{1,2,0:T(8,128)} %all-reduce.5.cloned.1.call-done), kind=kLoop, calls=%fused_computation.6 | loop fusion | flops 2097152 | bytes 16777216 | tf_op jit(solution)/shard_map/div | solution.py:32
  631.6 2.0 constant_dynamic-slice_fusion
  633.6 6.1 fusion
  (12 shorter events, 0.1 us)
Async XLA Ops:
  7.2 108.3 %all-gather.2.cloned.1.call-start = ((), (), s32[]{:S(2)}) async-start(), calls=%async_computation | async-start | bytes 8650752 | tf_op jit(solution)/shard_map/all_gather | solution.py:24
  7.9 278.1 %all-reduce.3.cloned.1.call-start = ((), (), s32[]{:S(2)}) async-start(), calls=%async_computation.1 | async-start | bytes 262144 | tf_op jit(solution)/shard_map/psum | solution.py:29
  8.0 324.8 %copy-start.2 = (bf16[1,4,32,8192]{3,2,1,0:T(8,128)(2,1)S(1)}, bf16[1,4,32,8192]{3,2,1,0:T(8,128)(2,1)}, u32[]{:S(2)}) copy-start(bf16[1,4,32,8192]{3,2,1,0:T(8,128)(2,1)} %param.3) | copy-start | bytes 6291460
  150.9 471.9 %all-reduce.5.cloned.1.call-start = ((), (), s32[]{:S(2)}) async-start(), calls=%async_computation.2 | async-start | bytes 16777216 | tf_op jit(solution)/shard_map/psum | solution.py:32
  622.9 10.7 %copy-start = (f32[1,4,32,8192]{3,2,1,0:T(8,128)S(1)}, f32[1,4,32,8192]{3,2,1,0:T(8,128)}, u32[]{:S(2)}) copy-start(f32[1,4,32,8192]{3,2,1,0:T(8,128)} %param.4) | copy-start | bytes 12582916
  622.9 10.7 %copy-start.1 = (f32[4,8192,64]{1,2,0:T(8,128)S(1)}, f32[4,8192,64]{1,2,0:T(8,128)}, u32[]{:S(2)}) copy-start(f32[4,8192,64]{1,2,0:T(8,128)} %all-reduce.5.cloned.1.call-done) | copy-start | bytes 25165828
Sparse Core Ops, SparseCore 0:
  10.5 104.9 all-gather.1
  151.1 134.9 all-reduce.2
  343.5 279.2 all-reduce.4
where the time goes:
time: 647 us; the launch traced here: 646 us
  waiting for transfers between devices  522 us (81%)
  other arithmetic  55.1 us (9%)
  matrix products  28.5 us (4%)
  blocking collectives  23.9 us (4%)
  between operations  13.8 us (2%)
    psum x1, waiting for transfers between devices, body(): q_all = lax.psum(term, ('dp', 'rows')) / groups  279 us
    psum x1, waiting for transfers between devices, body(): gram = lax.psum(local_gram, 'rows')  135 us
    all_gather x1, waiting for transfers between devices, body(): lax.all_gather(q_prev, 'rows', axis=1, tiled=True)  107 us
    psum x1, blocking collectives, body(): left = lax.psum(partial_left, 'dp') / groups  23.9 us
    another operation x4, other arithmetic, orthonormal(): jnp.linalg.cholesky(gram + (0.0001 * trace / gram.shape[1])[:, None, None...  23.6 us
    another operation x3, other arithmetic, orthonormal(): jax.scipy.linalg.solve_triangular(low, rhs, lower=True)  19.8 us
  transfers between devices with their start and end apart: 3, of which 3 were waited for; matrix products, arithmetic and copies ran while one was open for 0% of the time, Pallas kernels for 0%

commit v1 on v0

v1 whole, which is shorter than its diff:
```python
import jax
import jax.numpy as jnp
from jax import lax
from jax.experimental import pallas as pl
from jax.experimental.pallas import tpu as pltpu
from jax.sharding import PartitionSpec as P

MESH = pl.DeviceIdType.MESH
HIGHEST = lax.Precision.HIGHEST
NX, NY, NZ = 4, 4, 8
MATS, ROWS, RANK, GROUPS = 4, 32, 64, 8
BLOCK = 128
CHUNK = NX * 2 * BLOCK
DAMP = 0.0001

NN = (((1,), (0,)), ((), ()))
NT = (((1,), (1,)), ((), ()))

IN_ORDER = (4, 3, 5, 2, 6, 1, 7, 0)
OUT_ORDER = (0, 1, 7, 2, 6, 3, 5, 4)
PEERS = tuple((t, dx) for t in OUT_ORDER for dx in range(NX) if (t, dx) != (0, 0))


def dot(a, b, dims=NN):
    return lax.dot_general(a, b, dims, precision=HIGHEST, preferred_element_type=jnp.float32)


def inverse_factor(gram):
    n = RANK
    row = lax.broadcasted_iota(jnp.int32, (n, n), 0)
    col = lax.broadcasted_iota(jnp.int32, (n, n), 1)
    eye = jnp.where(row == col, 1.0, 0.0).astype(jnp.float32)
    trace = jnp.sum(gram * eye, axis=(0, 1), keepdims=True)
    full = jnp.concatenate([gram + (DAMP / n) * trace * eye, eye], axis=1)
    strips = [full[8 * i : 8 * i + 8] for i in range(n // 8)]
    sub = lax.broadcasted_iota(jnp.int32, (8, 2 * n), 0)
    scales = []
    for b in range(n // 8):
        live = range(b, n // 8)
        cols = {
            (i, j): jnp.broadcast_to(strips[i][:, 8 * b + j : 8 * b + j + 1], (8, 2 * n))
            for i in live
            for j in range(8)
        }
        scale = jnp.zeros((8, 2 * n), jnp.float32)
        for j in range(8):
            pivot = jnp.broadcast_to(cols[b, j][j : j + 1], (8, 2 * n))
            inv = 1.0 / pivot
            scale = jnp.where(sub == j, lax.rsqrt(pivot), scale)
            factor = {i: cols[i, j] for i in live}
            factor[b] = jnp.where(sub > j, factor[b], 0.0)
            lead = jnp.broadcast_to(strips[b][j : j + 1], (8, 2 * n)) * inv
            heads = {q: jnp.broadcast_to(cols[b, q][j : j + 1], (8, 2 * n)) * inv for q in range(j + 1, 8)}
            for i in live:
                strips[i] = strips[i] - factor[i] * lead
                for q in range(j + 1, 8):
                    cols[i, q] = cols[i, q] - factor[i] * heads[q]
        scales.append(scale)
    done = jnp.concatenate([s * c for s, c in zip(strips, scales)], axis=0)
    return done[:, n:]


def kernel(
    grads, errors, q_prev, q_out, e_out,
    g_in, e_in, q_in, merged, summed, pass_up, pass_dn, fin_up, fin_dn, mean, meant, q_all,
    acc, half_out, half_in, left, block_out, approx,
    ld_sem, q_sem, core_s, core_r, pass_s, pass_r, fin_s, fin_r, m_s, m_r, qz_s, qz_r, qx_s, qx_r,
    h_s, h_r, l_s, l_r, lc_s, lc_r, a_s, a_r, y_s, y_r, rel_s, rel_r, ac_s, ac_r, out_sem,
):
    d, r = lax.axis_index("dp"), lax.axis_index("rows")
    y, k = d // 2, d % 2
    z, x = r // NX, r % NX
    other = 1 - k
    y_up, y_dn, y_far = (y + 1) % NY, (y + 3) % NY, (y + 2) % NY
    partner = (y * 2 + other, r)
    up = (y_up * 2 + k, r)
    down = (y_dn * 2 + k, r)

    def peer(t, dx):
        return (d, ((z + t) % NZ) * NX + (x + dx) % NX)

    def zat(t):
        return (z + t) % NZ

    def xat(dx):
        return (x + dx) % NX

    sends = []

    def send(src, dst, ss, rs, to):
        copy = pltpu.make_async_remote_copy(
            src_ref=src, dst_ref=dst, send_sem=ss, recv_sem=rs, device_id=to, device_id_type=MESH
        )
        copy.start()
        sends.append(copy)
        return copy

    loads = {}
    q_load = pltpu.make_async_copy(q_prev.at[y, pl.ds(pl.multiple_of(k * BLOCK, BLOCK), BLOCK)], q_in, q_sem)
    q_load.start()
    for n, t in enumerate(IN_ORDER):
        at = pl.ds(pl.multiple_of(zat(t) * CHUNK, CHUNK), CHUNK)
        loads[n] = (
            pltpu.make_async_copy(grads.at[0, :, :, at], g_in.at[zat(t)], ld_sem.at[0, n]),
            pltpu.make_async_copy(errors.at[0, :, :, at], e_in.at[zat(t)], ld_sem.at[1, n]),
        )
        for load in loads[n]:
            load.start()

    barrier = pltpu.get_barrier_semaphore()
    for to in [partner, up, down] + [peer(t, dx) for t, dx in PEERS]:
        pl.semaphore_signal(barrier, inc=1, device_id=to, device_id_type=MESH)
    q_load.wait()
    q_all[z, x] = jnp.transpose(q_in[...])
    pl.semaphore_wait(barrier, 3 + len(PEERS))

    qz = [
        send(q_all.at[z, x], q_all.at[z, x], qz_s.at[t], qz_r.at[t], peer(t, 0)) for t in OUT_ORDER[1:]
    ]

    core, passes, finals, q_x = {}, {}, {}, []

    def four(c):
        return pl.ds(pl.multiple_of(c * NX, NX), NX)

    def merge(n):
        c = zat(IN_ORDER[n])
        for load in loads[n]:
            load.wait()

        def one(m, _):
            for j in range(2 * NX):
                cols = slice(j * BLOCK, (j + 1) * BLOCK)
                merged[m, j % 2, c * NX + j // 2] = g_in[c, m, :, cols].astype(jnp.float32) + e_in[c, m, :, cols]
            return 0

        lax.fori_loop(0, MATS, one, 0)
        core[n] = send(merged.at[:, other, four(c)], summed.at[:, four(c)], core_s.at[n], core_r.at[n], partner)

    def pair_sum(n):
        c = zat(IN_ORDER[n])
        core[n].wait_recv()

        def one(m, _):
            for j in range(NX):
                summed[m, c * NX + j] += merged[m, k, c * NX + j]
            return 0

        lax.fori_loop(0, MATS, one, 0)
        passes[n] = (
            send(summed.at[y_far, pl.ds(c * NX, 2)], pass_up.at[c], pass_s.at[0, n], pass_r.at[0, n], up),
            send(summed.at[y_far, pl.ds(c * NX + 2, 2)], pass_dn.at[c], pass_s.at[1, n], pass_r.at[1, n], down),
        )

    def pass_on(n):
        c = zat(IN_ORDER[n])
        for copy in passes[n]:
            copy.wait_recv()
        for j in range(2):
            summed[y_up, c * NX + j] += pass_up[c, j]
            summed[y_dn, c * NX + 2 + j] += pass_dn[c, j]
        finals[n] = (
            send(summed.at[y_up, four(c)], fin_up.at[c], fin_s.at[0, n], fin_r.at[0, n], up),
            send(summed.at[y_dn, four(c)], fin_dn.at[c], fin_s.at[1, n], fin_r.at[1, n], down),
        )

    mean_sent = {}

    def total(n):
        t = IN_ORDER[n]
        c = zat(t)
        for copy in finals[n]:
            copy.wait_recv()
        for j in range(NX):
            mean[c, j] = summed[y, c * NX + j] + fin_up[c, j] + fin_dn[c, j]
        for dx in range(NX):
            if (t, dx) == (0, 0):
                meant[z, x] = mean[z, x]
            else:
                mean_sent[t, dx] = send(
                    mean.at[c, xat(dx)], meant.at[z, x], m_s.at[t, dx], m_r.at[t, dx], peer(t, dx)
                )

    def spread_q():
        for copy in qz:
            copy.wait_recv()
        for dx in range(1, NX):
            q_x.append(send(q_all.at[:, x], q_all.at[:, x], qx_s.at[dx], qx_r.at[dx], peer(0, dx)))

    def project(n):
        c = zat(IN_ORDER[n])
        part = dot(mean[c, 0], q_all[c, 0], NT)
        for j in range(1, NX):
            part = part + dot(mean[c, j], q_all[c, j], NT)
        if n == 0:
            acc[...] = part
        else:
            acc[...] += part

    steps = len(IN_ORDER)
    for n in range(steps + 4):
        if n < steps:
            merge(n)
        if 0 <= n - 1 < steps:
            pair_sum(n - 1)
        if 0 <= n - 2 < steps:
            pass_on(n - 2)
        if n == 5:
            spread_q()
        if 0 <= n - 4 < steps:
            total(n - 4)
        if n == steps + 2:
            for copy in q_x:
                copy.wait_recv()
            for i in range(steps - 1):
                project(i)
    project(steps - 1)

    half_out[0] = acc[:16]
    half_out[1] = acc[16:]
    swap = send(half_out.at[other], half_in, h_s, h_r, partner)
    swap.wait_recv()
    mine = (half_out[k] + half_in[...]) * (1.0 / GROUPS)
    left[z, x, k] = jnp.concatenate([mine[:8], mine[8:]], axis=1)
    spread = [
        send(left.at[z, x, k], left.at[z, x, k], l_s.at[t, dx], l_r.at[t, dx], peer(t, dx)) for t, dx in PEERS
    ]
    for copy in spread:
        copy.wait_recv()
    cross = send(left.at[:, :, k], left.at[:, :, k], lc_s, lc_r, partner)
    for copy in mean_sent.values():
        copy.wait_recv()
    cross.wait_recv()

    parts = [left[:, :, i].reshape(NZ * NX * 8, BLOCK) for i in range(2)]
    turned = [jnp.transpose(p) for p in parts]
    square = dot(turned[0], parts[0]) + dot(turned[1], parts[1])
    gram = square[:RANK, :RANK] + square[RANK:, RANK:]
    inv = inverse_factor(gram)

    def rows_of(i, j):
        return pl.ds(16 * i + 8 * j, 8)

    prod = [
        sum(dot(turned[i], meant[:, :, rows_of(i, j)].reshape(NZ * NX * 8, BLOCK)) for i in range(2))
        for j in range(2)
    ]
    proj = prod[0][:RANK] + prod[1][RANK:]
    q_mine = dot(inv, proj) * (1.0 / GROUPS)
    solved = dot(jnp.transpose(inv), q_mine)
    zero = jnp.zeros((RANK, BLOCK), jnp.float32)
    wide = [jnp.concatenate([solved, zero], axis=0), jnp.concatenate([zero, solved], axis=0)]
    approx[k, y, 32] = q_mine[:32]
    approx[k, y, 33] = q_mine[32:]
    for i in range(2):
        for j in range(2):
            block_out[:, :, rows_of(i, j)] = dot(parts[i], wide[j]).reshape(NZ, NX, 8, BLOCK)

    blocks = {
        (t, dx): send(
            block_out.at[zat(t), xat(dx)], approx.at[k, y, r], a_s.at[t, dx], a_r.at[t, dx], peer(t, dx)
        )
        for t, dx in PEERS
    }
    approx[k, y, r] = block_out[z, x]

    direct, relay, crossed, outs = {}, {}, {}, []

    def places(n):
        if n == steps:
            return pl.ds(32, 2), pl.ds(32, 1), pl.ds(33, 1)
        c = (z + NZ - OUT_ORDER[n]) % NZ
        return four(c), pl.ds(c * NX, 2), pl.ds(c * NX + 2, 2)

    def share(n):
        if n < steps:
            for dx in range(NX):
                if (OUT_ORDER[n], dx) != (0, 0):
                    blocks[OUT_ORDER[n], dx].wait_recv()
        at = places(n)[0]
        here = approx.at[k, y, at]
        direct[n] = (
            send(here, here, y_s.at[0, n], y_r.at[0, n], up),
            send(here, here, y_s.at[1, n], y_r.at[1, n], down),
        )

    def pass_along(n):
        _, first, second = places(n)
        for copy in direct[n]:
            copy.wait_recv()
        from_dn, from_up = approx.at[k, y_dn, first], approx.at[k, y_up, second]
        relay[n] = (
            send(from_dn, from_dn, rel_s.at[0, n], rel_r.at[0, n], up),
            send(from_up, from_up, rel_s.at[1, n], rel_r.at[1, n], down),
        )

    def over(n):
        for copy in relay[n]:
            copy.wait_recv()
        here = approx.at[k, :, places(n)[0]]
        crossed[n] = send(here, here, ac_s.at[n], ac_r.at[n], partner)

    def finish(n):
        crossed[n].wait_recv()
        if n == steps:
            for m in range(MATS):
                for h in range(2):
                    q_out[m, h * BLOCK : (h + 1) * BLOCK] = jnp.transpose(
                        approx[h, m, 32:34].reshape(RANK, BLOCK)
                    )
            return
        c = (z + NZ - OUT_ORDER[n]) % NZ

        def one(m, _):
            for j in range(2 * NX):
                b = c * NX + j // 2
                e_in[c, m, :, j * BLOCK : (j + 1) * BLOCK] = merged[m, j % 2, b] - approx[j % 2, m, b]
            return 0

        lax.fori_loop(0, MATS, one, 0)
        at = pl.ds(pl.multiple_of(c * CHUNK, CHUNK), CHUNK)
        out = pltpu.make_async_copy(e_in.at[c], e_out.at[0, :, :, at], out_sem.at[n])
        out.start()
        outs.append(out)

    order = [steps] + list(range(steps))
    for n in range(len(order) + 3):
        if n < len(order):
            share(order[n])
        if 0 <= n - 1 < len(order):
            pass_along(order[n - 1])
        if 0 <= n - 2 < len(order):
            over(order[n - 2])
        if 0 <= n - 3 < len(order):
            finish(order[n - 3])

    for copy in sends:
        copy.wait_send()
    for out in outs:
        out.wait()


def body(grads, errors, q_prev):
    f32 = jnp.float32
    dma = pltpu.SemaphoreType.DMA
    blocks = NZ * NX
    q_new, errors_new = pl.pallas_call(
        kernel,
        out_shape=(
            jax.ShapeDtypeStruct((MATS, 2 * BLOCK, RANK), f32),
            jax.ShapeDtypeStruct(errors.shape, f32),
        ),
        in_specs=[pl.BlockSpec(memory_space=pl.ANY)] * 3,
        out_specs=(pl.BlockSpec(memory_space=pltpu.VMEM), pl.BlockSpec(memory_space=pl.ANY)),
        scratch_shapes=[
            pltpu.VMEM((NZ, MATS, ROWS, CHUNK), grads.dtype),
            pltpu.VMEM((NZ, MATS, ROWS, CHUNK), f32),
            pltpu.VMEM((BLOCK, RANK), f32),
            pltpu.VMEM((MATS, 2, blocks, ROWS, BLOCK), f32),
            pltpu.VMEM((MATS, blocks, ROWS, BLOCK), f32),
            pltpu.VMEM((NZ, 2, ROWS, BLOCK), f32),
            pltpu.VMEM((NZ, 2, ROWS, BLOCK), f32),
            pltpu.VMEM((NZ, NX, ROWS, BLOCK), f32),
            pltpu.VMEM((NZ, NX, ROWS, BLOCK), f32),
            pltpu.VMEM((NZ, NX, ROWS, BLOCK), f32),
            pltpu.VMEM((NZ, NX, ROWS, BLOCK), f32),
            pltpu.VMEM((NZ, NX, RANK, BLOCK), f32),
            pltpu.VMEM((ROWS, RANK), f32),
            pltpu.VMEM((2, ROWS // 2, RANK), f32),
            pltpu.VMEM((ROWS // 2, RANK), f32),
            pltpu.VMEM((NZ, NX, 2, 8, BLOCK), f32),
            pltpu.VMEM((NZ, NX, ROWS, BLOCK), f32),
            pltpu.VMEM((2, MATS, blocks + 2, ROWS, BLOCK), f32),
            dma((2, 8)), dma,
            dma((8,)), dma((8,)),
            dma((2, 8)), dma((2, 8)),
            dma((2, 8)), dma((2, 8)),
            dma((NZ, NX)), dma((NZ, NX)),
            dma((NZ,)), dma((NZ,)),
            dma((NX,)), dma((NX,)),
            dma, dma,
            dma((NZ, NX)), dma((NZ, NX)),
            dma, dma,
            dma((NZ, NX)), dma((NZ, NX)),
            dma((2, 9)), dma((2, 9)),
            dma((2, 9)), dma((2, 9)),
            dma((9,)), dma((9,)),
            dma((8,)),
        ],
        name="powersgd",
        compiler_params=pltpu.CompilerParams(
            collective_id=0, has_side_effects=True, vmem_limit_bytes=48 << 20
        ),
    )(grads, errors, q_prev)
    return q_new, errors_new


def solution(mesh):
    return jax.shard_map(
        body,
        mesh=mesh,
        in_specs=(P("dp", None, "rows", None), P("dp", None, "rows", None), P(None, "rows", None)),
        out_specs=(P(None, "rows", None), P("dp", None, "rows", None)),
        check_vma=False,
    )
```

time: 647 us -> 101 us (0.16)
  waiting for transfers between devices: 522 us -> 0 us
  Pallas kernels: 0 us -> 91.8 us
  other arithmetic: 55.1 us -> 0 us
  matrix products: 28.5 us -> 0 us
  blocking collectives: 23.9 us -> 0 us
  between operations: 13.8 us -> 0.65 us
    psum x2 -> x0, waiting for transfers between devices: 414 us -> none  [the longest x1 279 us: body(): q_all = lax.psum(term, ('dp', 'rows')) / groups]
    all_gather x1 -> x0, waiting for transfers between devices: 107 us -> none  [body(): lax.all_gather(q_prev, 'rows', axis=1, tiled=True)]
    pallas_call x0 -> x1, Pallas kernels: none -> 91.8 us  [body(): pl.pallas_call(kernel, out_shape=(jax.ShapeDtypeStruct((MATS, 2 * BLOCK,...]
    another operation x7 -> x0, other arithmetic: 43.4 us -> none  [the longest x4 23.6 us: orthonormal(): jnp.linalg.cholesky(gram + (0.0001 * trace / gram.shape[1])[:, None, None...]
    dot_general x4 -> x0, matrix products: 28.3 us -> none  [the longest x1 10.6 us: body(): jnp.einsum('mrc,mrk->mck', merged, ortho, precision=lax.Precision.HIGHEST)]
    psum x1 -> x0, blocking collectives: 23.9 us -> none  [body(): left = lax.psum(partial_left, 'dp') / groups]
    div x3 -> x0, other arithmetic: 9.71 us -> none  [the longest x1 8.71 us: body(): q_all = lax.psum(term, ('dp', 'rows')) / groups]
    unnamed x6 -> x4, local copies, waits for them, and re-layouts: 0.01 us -> 7.34 us
  transfers between devices with their start and end apart: 3 -> 0, of which waited for: 3 -> 0; matrix products, arithmetic and copies ran while one was open for 0% -> 0% of each run, Pallas kernels for 0% -> 0%
where the time goes in v1:
time: 101 us
  Pallas kernels  91.8 us (91%)
  local copies, waits for them, and re-layouts  8.22 us (8%)
    pallas_call x1, Pallas kernels, body(): pl.pallas_call(kernel, out_shape=(jax.ShapeDtypeStruct((MATS, 2 * BLOCK,...  91.8 us
    unnamed x4, local copies, waits for them, and re-layouts  7.34 us

profile of v1, /device:TPU:1, one launch (start us, length us, event | category | flops | bytes accessed | tf_op | source)
XLA Modules:
  0.0 100.7 jit_solution(5215092846083376791)
XLA Ops:
  0.6 1.1 %copy.5.q_prev = f32[4,256,64]{2,1,0:T(8,128)S(1)} copy(f32[4,256,64]{1,2,0:T(8,128)} %param.5) | data formatting | bytes 524288 | tf_op args[2]
  1.8 0.0 copy-start
  1.8 1.6 %copy-done = bf16[1,4,32,8192]{3,2,1,0:T(8,128)(2,1)S(1)} copy-done((bf16[1,4,32,8192]{3,2,1,0:T(8,128)(2,1)S(1)}, bf16[1,4,32,8192]{3,2,1,0:T(8,128)(2,1)}, u32[]{:S(2)}) %copy-start) | copy-done | bytes 2097176
  3.4 91.8 %powersgd.1 = (f32[4,256,64]{2,1,0:T(8,128)S(1)}, f32[1,4,32,8192]{3,2,1,0:T(8,128)}) custom-call(bf16[1,4,32,8192]{3,2,1,0:T(8,128)(2,1)S(1)} %copy-done, f32[1,4,32,8192]{3,2,1,0:T(8,128)} %errors.1, f32[4,256,64]{2,1,0:T(8,128)S(1)} %copy.5.q_prev), custom_call_target="tpu_custom_call" | custom-call | tf_op jit(solution)/shard_map/powersgd/pallas_call | solution.py:347
  95.2 0.9 copy.6
  96.1 4.6 %copy.8 = f32[1,4,32,8192]{3,2,1,0:T(8,128)} copy(f32[1,4,32,8192]{3,2,1,0:T(8,128)} %get-tuple-element.7) | data formatting | bytes 8388608
Async XLA Ops:
  1.8 1.6 %copy-start = (bf16[1,4,32,8192]{3,2,1,0:T(8,128)(2,1)S(1)}, bf16[1,4,32,8192]{3,2,1,0:T(8,128)(2,1)}, u32[]{:S(2)}) copy-start(bf16[1,4,32,8192]{3,2,1,0:T(8,128)(2,1)} %grads.1) | copy-start | bytes 6291460

commit v2 on v1

--- a/solution.py
+++ b/solution.py
@@ -18,6 +18,7 @@
 
 IN_ORDER = (4, 3, 5, 2, 6, 1, 7, 0)
 OUT_ORDER = (0, 1, 7, 2, 6, 3, 5, 4)
+ONWARD = {0: (1, 7), 1: (2,), 2: (3,), 3: (4,), 4: (), 5: (), 6: (5,), 7: (6,)}
 PEERS = tuple((t, dx) for t in OUT_ORDER for dx in range(NX) if (t, dx) != (0, 0))
 
 
@@ -62,10 +63,10 @@
 
 def kernel(
     grads, errors, q_prev, q_out, e_out,
-    g_in, e_in, q_in, merged, summed, pass_up, pass_dn, fin_up, fin_dn, mean, meant, q_all,
-    acc, half_out, half_in, left, block_out, approx,
+    g_in, e_in, merged, summed, pass_up, pass_dn, fin_up, fin_dn, mean, meant, q_all,
+    acc, half_out, half_in, left, v_all, block_out, approx,
     ld_sem, q_sem, core_s, core_r, pass_s, pass_r, fin_s, fin_r, m_s, m_r, qz_s, qz_r, qx_s, qx_r,
-    h_s, h_r, l_s, l_r, lc_s, lc_r, a_s, a_r, y_s, y_r, rel_s, rel_r, ac_s, ac_r, out_sem,
+    h_s, h_r, v_s, v_r, l_s, l_r, lc_s, lc_r, a_s, a_r, y_s, y_r, rel_s, rel_r, ac_s, ac_r,
 ):
     d, r = lax.axis_index("dp"), lax.axis_index("rows")
     y, k = d // 2, d % 2
@@ -85,6 +86,11 @@
     def xat(dx):
         return (x + dx) % NX
 
+    def ring(buf, ss, rs, copies, t):
+        here = buf((z + NZ - t) % NZ)
+        for u in ONWARD[t]:
+            copies[u] = send(here, here, ss.at[u], rs.at[u], peer(1 if u <= 4 else 7, 0))
+
     sends = []
 
     def send(src, dst, ss, rs, to):
@@ -96,7 +102,9 @@
         return copy
 
     loads = {}
-    q_load = pltpu.make_async_copy(q_prev.at[y, pl.ds(pl.multiple_of(k * BLOCK, BLOCK), BLOCK)], q_in, q_sem)
+    q_load = pltpu.make_async_copy(
+        q_prev.at[y, :, pl.ds(pl.multiple_of(k * BLOCK, BLOCK), BLOCK)], q_all.at[z, x], q_sem
+    )
     q_load.start()
     for n, t in enumerate(IN_ORDER):
         at = pl.ds(pl.multiple_of(zat(t) * CHUNK, CHUNK), CHUNK)
@@ -110,15 +118,7 @@
     barrier = pltpu.get_barrier_semaphore()
     for to in [partner, up, down] + [peer(t, dx) for t, dx in PEERS]:
         pl.semaphore_signal(barrier, inc=1, device_id=to, device_id_type=MESH)
-    q_load.wait()
-    q_all[z, x] = jnp.transpose(q_in[...])
-    pl.semaphore_wait(barrier, 3 + len(PEERS))
-
-    qz = [
-        send(q_all.at[z, x], q_all.at[z, x], qz_s.at[t], qz_r.at[t], peer(t, 0)) for t in OUT_ORDER[1:]
-    ]
-
-    core, passes, finals, q_x = {}, {}, {}, []
+    core, passes, finals, q_z, q_x = {}, {}, {}, {}, {}
 
     def four(c):
         return pl.ds(pl.multiple_of(c * NX, NX), NX)
@@ -135,6 +135,9 @@
             return 0
 
         lax.fori_loop(0, MATS, one, 0)
+
+    def swap_cores(n):
+        c = zat(IN_ORDER[n])
         core[n] = send(merged.at[:, other, four(c)], summed.at[:, four(c)], core_s.at[n], core_r.at[n], partner)
 
     def pair_sum(n):
@@ -181,11 +184,20 @@
                     mean.at[c, xat(dx)], meant.at[z, x], m_s.at[t, dx], m_r.at[t, dx], peer(t, dx)
                 )
 
-    def spread_q():
-        for copy in qz:
-            copy.wait_recv()
-        for dx in range(1, NX):
-            q_x.append(send(q_all.at[:, x], q_all.at[:, x], qx_s.at[dx], qx_r.at[dx], peer(0, dx)))
+    def spread_q(t):
+        if t > 0:
+            q_z[t].wait_recv()
+        ring(lambda c: q_all.at[c, x], qz_s, qz_r, q_z, t)
+        here = q_all.at[(z + NZ - t) % NZ, x]
+        for dx in (1, 3):
+            q_x[t, dx] = send(here, here, qx_s.at[t, dx], qx_r.at[t, dx], peer(0, dx))
+
+    def relay_q(t):
+        for dx in (1, 3):
+            q_x[t, dx].wait_recv()
+        dx = 1 if t < 4 else 3
+        here = q_all.at[(z + NZ - t) % NZ, xat(NX - dx)]
+        q_x[t, 2] = send(here, here, qx_s.at[t, 2], qx_r.at[t, 2], peer(0, dx))
 
     def project(n):
         c = zat(IN_ORDER[n])
@@ -198,22 +210,29 @@
             acc[...] += part
 
     steps = len(IN_ORDER)
-    for n in range(steps + 4):
-        if n < steps:
-            merge(n)
-        if 0 <= n - 1 < steps:
-            pair_sum(n - 1)
-        if 0 <= n - 2 < steps:
-            pass_on(n - 2)
-        if n == 5:
-            spread_q()
-        if 0 <= n - 4 < steps:
-            total(n - 4)
-        if n == steps + 2:
-            for copy in q_x:
-                copy.wait_recv()
-            for i in range(steps - 1):
-                project(i)
+    for n in range(steps):
+        merge(n)
+    q_load.wait()
+    pl.semaphore_wait(barrier, 3 + len(PEERS))
+
+    for n in range(steps):
+        swap_cores(n)
+    spread_q(0)
+    plan = [
+        (pair_sum, 0), (pair_sum, 1), (pair_sum, 2), (pair_sum, 3), (spread_q, 1), (spread_q, 7),
+        (pair_sum, 4), (pair_sum, 5), (pair_sum, 6), (pair_sum, 7), (relay_q, 0), (pass_on, 0), (pass_on, 1),
+        (spread_q, 2), (spread_q, 6), (relay_q, 1), (relay_q, 7), (pass_on, 2), (pass_on, 3), (total, 0),
+        (spread_q, 3), (spread_q, 5), (relay_q, 2), (relay_q, 6), (pass_on, 4), (total, 1), (pass_on, 5),
+        (total, 2), (spread_q, 4), (relay_q, 3), (relay_q, 5), (pass_on, 6), (total, 3), (pass_on, 7),
+        (total, 4), (relay_q, 4), (total, 5), (total, 6),
+    ]
+    for step, n in plan:
+        step(n)
+    for t in range(NZ):
+        q_x[t, 2].wait_recv()
+    for n in range(steps - 1):
+        project(n)
+    total(steps - 1)
     project(steps - 1)
 
     half_out[0] = acc[:16]
@@ -248,23 +267,32 @@
     proj = prod[0][:RANK] + prod[1][RANK:]
     q_mine = dot(inv, proj) * (1.0 / GROUPS)
     solved = dot(jnp.transpose(inv), q_mine)
+    v_all[z] = solved
+    v_sent = {}
     zero = jnp.zeros((RANK, BLOCK), jnp.float32)
-    wide = [jnp.concatenate([solved, zero], axis=0), jnp.concatenate([zero, solved], axis=0)]
+    rows = left[z].reshape(NX * 2 * 8, BLOCK)
     approx[k, y, 32] = q_mine[:32]
     approx[k, y, 33] = q_mine[32:]
-    for i in range(2):
+
+    def expand(n):
+        t = OUT_ORDER[n]
+        c = (z + NZ - t) % NZ
+        if n > 0:
+            v_sent[t].wait_recv()
+        ring(lambda c: v_all.at[c], v_s, v_r, v_sent, t)
+        v = v_all[c]
         for j in range(2):
-            block_out[:, :, rows_of(i, j)] = dot(parts[i], wide[j]).reshape(NZ, NX, 8, BLOCK)
-
-    blocks = {
-        (t, dx): send(
-            block_out.at[zat(t), xat(dx)], approx.at[k, y, r], a_s.at[t, dx], a_r.at[t, dx], peer(t, dx)
-        )
-        for t, dx in PEERS
-    }
-    approx[k, y, r] = block_out[z, x]
-
-    direct, relay, crossed, outs = {}, {}, {}, []
+            wide = jnp.concatenate([v, zero] if j == 0 else [zero, v], axis=0)
+            got = dot(rows, wide).reshape(NX, 2, 8, BLOCK)
+            for i in range(2):
+                block_out[c, :, rows_of(i, j)] = got[:, i]
+        for dx in range(1, NX):
+            blocks[n, dx] = send(
+                block_out.at[c, xat(dx)], approx.at[k, y, c * NX + x], a_s.at[t, dx], a_r.at[t, dx], peer(0, dx)
+            )
+        approx[k, y, c * NX + x] = block_out[c, x]
+
+    blocks, direct, relay, crossed = {}, {}, {}, {}
 
     def places(n):
         if n == steps:
@@ -274,9 +302,8 @@
 
     def share(n):
         if n < steps:
-            for dx in range(NX):
-                if (OUT_ORDER[n], dx) != (0, 0):
-                    blocks[OUT_ORDER[n], dx].wait_recv()
+            for dx in range(1, NX):
+                blocks[n, dx].wait_recv()
         at = places(n)[0]
         here = approx.at[k, y, at]
         direct[n] = (
@@ -305,39 +332,33 @@
         if n == steps:
             for m in range(MATS):
                 for h in range(2):
-                    q_out[m, h * BLOCK : (h + 1) * BLOCK] = jnp.transpose(
-                        approx[h, m, 32:34].reshape(RANK, BLOCK)
-                    )
+                    q_out[m, :, h * BLOCK : (h + 1) * BLOCK] = approx[h, m, 32:34].reshape(RANK, BLOCK)
             return
         c = (z + NZ - OUT_ORDER[n]) % NZ
 
         def one(m, _):
             for j in range(2 * NX):
                 b = c * NX + j // 2
-                e_in[c, m, :, j * BLOCK : (j + 1) * BLOCK] = merged[m, j % 2, b] - approx[j % 2, m, b]
+                at = pl.ds(pl.multiple_of(c * CHUNK + j * BLOCK, BLOCK), BLOCK)
+                e_out[0, m, :, at] = merged[m, j % 2, b] - approx[j % 2, m, b]
             return 0
 
         lax.fori_loop(0, MATS, one, 0)
-        at = pl.ds(pl.multiple_of(c * CHUNK, CHUNK), CHUNK)
-        out = pltpu.make_async_copy(e_in.at[c], e_out.at[0, :, :, at], out_sem.at[n])
-        out.start()
-        outs.append(out)
-
-    order = [steps] + list(range(steps))
-    for n in range(len(order) + 3):
-        if n < len(order):
-            share(order[n])
-        if 0 <= n - 1 < len(order):
-            pass_along(order[n - 1])
-        if 0 <= n - 2 < len(order):
-            over(order[n - 2])
-        if 0 <= n - 3 < len(order):
-            finish(order[n - 3])
+
+    Q = steps
+    plan = [
+        (expand, 0), (share, Q), (share, 0), (expand, 1), (expand, 2), (share, 1), (share, 2), (pass_along, Q),
+        (pass_along, 0), (expand, 3), (expand, 4), (share, 3), (share, 4), (pass_along, 1), (pass_along, 2),
+        (over, Q), (over, 0), (expand, 5), (expand, 6), (share, 5), (share, 6), (pass_along, 3), (pass_along, 4),
+        (over, 1), (over, 2), (expand, 7), (share, 7), (finish, Q), (finish, 0), (pass_along, 5), (pass_along, 6),
+        (over, 3), (over, 4), (finish, 1), (finish, 2), (pass_along, 7), (over, 5), (over, 6), (finish, 3),
+        (finish, 4), (over, 7), (finish, 5), (finish, 6), (finish, 7),
+    ]
+    for step, n in plan:
+        step(n)
 
     for copy in sends:
         copy.wait_send()
-    for out in outs:
-        out.wait()
 
 
 def body(grads, errors, q_prev):
@@ -347,15 +368,14 @@
     q_new, errors_new = pl.pallas_call(
         kernel,
         out_shape=(
-            jax.ShapeDtypeStruct((MATS, 2 * BLOCK, RANK), f32),
+            jax.ShapeDtypeStruct((MATS, RANK, 2 * BLOCK), f32),
             jax.ShapeDtypeStruct(errors.shape, f32),
         ),
-        in_specs=[pl.BlockSpec(memory_space=pl.ANY)] * 3,
-        out_specs=(pl.BlockSpec(memory_space=pltpu.VMEM), pl.BlockSpec(memory_space=pl.ANY)),
+        in_specs=[pl.BlockSpec(memory_space=pltpu.HBM)] * 3,
+        out_specs=(pl.BlockSpec(memory_space=pltpu.VMEM), pl.BlockSpec(memory_space=pltpu.VMEM)),
         scratch_shapes=[
             pltpu.VMEM((NZ, MATS, ROWS, CHUNK), grads.dtype),
             pltpu.VMEM((NZ, MATS, ROWS, CHUNK), f32),
-            pltpu.VMEM((BLOCK, RANK), f32),
             pltpu.VMEM((MATS, 2, blocks, ROWS, BLOCK), f32),
             pltpu.VMEM((MATS, blocks, ROWS, BLOCK), f32),
             pltpu.VMEM((NZ, 2, ROWS, BLOCK), f32),
@@ -369,6 +389,7 @@
             pltpu.VMEM((2, ROWS // 2, RANK), f32),
             pltpu.VMEM((ROWS // 2, RANK), f32),
             pltpu.VMEM((NZ, NX, 2, 8, BLOCK), f32),
+            pltpu.VMEM((NZ, RANK, BLOCK), f32),
             pltpu.VMEM((NZ, NX, ROWS, BLOCK), f32),
             pltpu.VMEM((2, MATS, blocks + 2, ROWS, BLOCK), f32),
             dma((2, 8)), dma,
@@ -377,22 +398,22 @@
             dma((2, 8)), dma((2, 8)),
             dma((NZ, NX)), dma((NZ, NX)),
             dma((NZ,)), dma((NZ,)),
-            dma((NX,)), dma((NX,)),
+            dma((NZ, NX)), dma((NZ, NX)),
             dma, dma,
+            dma((NZ,)), dma((NZ,)),
             dma((NZ, NX)), dma((NZ, NX)),
             dma, dma,
             dma((NZ, NX)), dma((NZ, NX)),
             dma((2, 9)), dma((2, 9)),
             dma((2, 9)), dma((2, 9)),
             dma((9,)), dma((9,)),
-            dma((8,)),
         ],
         name="powersgd",
         compiler_params=pltpu.CompilerParams(
-            collective_id=0, has_side_effects=True, vmem_limit_bytes=48 << 20
+            collective_id=0, has_side_effects=True, vmem_limit_bytes=46 << 20
         ),
-    )(grads, errors, q_prev)
-    return q_new, errors_new
+    )(grads, errors, jnp.swapaxes(q_prev, 1, 2))
+    return jnp.swapaxes(q_new, 1, 2), errors_new
 
 
 def solution(mesh):

time: 101 us -> 92.2 us (0.913)
  Pallas kernels: 91.8 us -> 86.1 us
  local copies, waits for them, and re-layouts: 8.22 us -> 5.25 us
    pallas_call x1, Pallas kernels: 91.8 us -> 86.1 us  [body(): pl.pallas_call(kernel, out_shape=(jax.ShapeDtypeStruct((MATS, RANK, 2 * B...]
    unnamed x4 -> x6, local copies, waits for them, and re-layouts: 7.34 us -> 5.25 us
where the time goes in v2:
time: 92.2 us; the launch traced here: 92 us
  Pallas kernels  86.1 us (93%)
  local copies, waits for them, and re-layouts  5.25 us (6%)
    pallas_call x1, Pallas kernels, body(): pl.pallas_call(kernel, out_shape=(jax.ShapeDtypeStruct((MATS, RANK, 2 * B...  86.1 us
    unnamed x6, local copies, waits for them, and re-layouts  5.25 us

profile of v2, /device:TPU:1, one launch (start us, length us, event | category | flops | bytes accessed | tf_op | source)
XLA Modules:
  0.0 92.0 jit_solution(13996617598817763826)
XLA Ops:
  0.6 0.0 copy-start
  0.6 1.6 %copy-done = bf16[1,4,32,8192]{3,2,1,0:T(8,128)(2,1)S(1)} copy-done((bf16[1,4,32,8192]{3,2,1,0:T(8,128)(2,1)S(1)}, bf16[1,4,32,8192]{3,2,1,0:T(8,128)(2,1)}, u32[]{:S(2)}) %copy-start) | copy-done | bytes 2097176
  2.2 0.0 copy-start.1
  2.2 0.9 %copy-done.1 = f32[4,256,64]{1,2,0:T(8,128)S(1)} copy-done((f32[4,256,64]{1,2,0:T(8,128)S(1)}, f32[4,256,64]{1,2,0:T(8,128)}, u32[]{:S(2)}) %copy-start.1) | copy-done | bytes 262168
  3.2 86.1 %powersgd.1 = (f32[4,64,256]{2,1,0:T(8,128)S(1)}, f32[1,4,32,8192]{3,2,1,0:T(8,128)S(1)}) custom-call(bf16[1,4,32,8192]{3,2,1,0:T(8,128)(2,1)S(1)} %copy-done, f32[1,4,32,8192]{3,2,1,0:T(8,128)} %errors.1, f32[4,64,256]{2,1,0:T(8,128)S(1)} %bitcast.2), custom_call_target="tpu_custom_call" | custom-call | tf_op jit(solution)/shard_map/powersgd/pallas_call | solution.py:368
  89.3 0.7 copy.7
  90.0 2.0 %copy.8 = f32[1,4,32,8192]{3,2,1,0:T(8,128)} copy(f32[1,4,32,8192]{3,2,1,0:T(8,128)S(1)} %get-tuple-element.9) | data formatting | bytes 8388608
Async XLA Ops:
  0.6 1.6 %copy-start = (bf16[1,4,32,8192]{3,2,1,0:T(8,128)(2,1)S(1)}, bf16[1,4,32,8192]{3,2,1,0:T(8,128)(2,1)}, u32[]{:S(2)}) copy-start(bf16[1,4,32,8192]{3,2,1,0:T(8,128)(2,1)} %grads.1) | copy-start | bytes 6291460
  2.2 0.9 %copy-start.1 = (f32[4,256,64]{1,2,0:T(8,128)S(1)}, f32[4,256,64]{1,2,0:T(8,128)}, u32[]{:S(2)}) copy-start(f32[4,256,64]{1,2,0:T(8,128)} %param.5) | copy-start | bytes 786436

commit v3 on v2

--- a/solution.py
+++ b/solution.py
@@ -16,10 +16,10 @@
 NN = (((1,), (0,)), ((), ()))
 NT = (((1,), (1,)), ((), ()))
 
-IN_ORDER = (4, 3, 5, 2, 6, 1, 7, 0)
-OUT_ORDER = (0, 1, 7, 2, 6, 3, 5, 4)
+ORDER = (0, 1, 7, 2, 6, 3, 5, 4)
 ONWARD = {0: (1, 7), 1: (2,), 2: (3,), 3: (4,), 4: (), 5: (), 6: (5,), 7: (6,)}
-PEERS = tuple((t, dx) for t in OUT_ORDER for dx in range(NX) if (t, dx) != (0, 0))
+ONWARD_FAR = {2: (3,), 3: (4,), 6: (5,)}
+PEERS = tuple((t, dx) for t in ORDER for dx in range(NX) if (t, dx) != (0, 0))
 
 
 def dot(a, b, dims=NN):
@@ -86,12 +86,16 @@
     def xat(dx):
         return (x + dx) % NX
 
-    def ring(buf, ss, rs, copies, t):
+    def ring(buf, ss, rs, copies, t, onward=ONWARD):
         here = buf((z + NZ - t) % NZ)
-        for u in ONWARD[t]:
+        for u in onward.get(t, ()):
             copies[u] = send(here, here, ss.at[u], rs.at[u], peer(1 if u <= 4 else 7, 0))
 
     sends = []
+
+    def flush():
+        while sends:
+            sends.pop(0).wait_send()
 
     def send(src, dst, ss, rs, to):
         copy = pltpu.make_async_remote_copy(
@@ -106,7 +110,7 @@
         q_prev.at[y, :, pl.ds(pl.multiple_of(k * BLOCK, BLOCK), BLOCK)], q_all.at[z, x], q_sem
     )
     q_load.start()
-    for n, t in enumerate(IN_ORDER):
+    for n, t in enumerate(ORDER):
         at = pl.ds(pl.multiple_of(zat(t) * CHUNK, CHUNK), CHUNK)
         loads[n] = (
             pltpu.make_async_copy(grads.at[0, :, :, at], g_in.at[zat(t)], ld_sem.at[0, n]),
@@ -116,7 +120,8 @@
             load.start()
 
     barrier = pltpu.get_barrier_semaphore()
-    for to in [partner, up, down] + [peer(t, dx) for t, dx in PEERS]:
+    near = [partner, up, down, peer(1, 0), peer(7, 0), peer(0, 1), peer(0, 3)]
+    for to in near:
         pl.semaphore_signal(barrier, inc=1, device_id=to, device_id_type=MESH)
     core, passes, finals, q_z, q_x = {}, {}, {}, {}, {}
 
@@ -124,7 +129,7 @@
         return pl.ds(pl.multiple_of(c * NX, NX), NX)
 
     def merge(n):
-        c = zat(IN_ORDER[n])
+        c = zat(ORDER[n])
         for load in loads[n]:
             load.wait()
 
@@ -137,11 +142,11 @@
         lax.fori_loop(0, MATS, one, 0)
 
     def swap_cores(n):
-        c = zat(IN_ORDER[n])
+        c = zat(ORDER[n])
         core[n] = send(merged.at[:, other, four(c)], summed.at[:, four(c)], core_s.at[n], core_r.at[n], partner)
 
     def pair_sum(n):
-        c = zat(IN_ORDER[n])
+        c = zat(ORDER[n])
         core[n].wait_recv()
 
         def one(m, _):
@@ -156,7 +161,7 @@
         )
 
     def pass_on(n):
-        c = zat(IN_ORDER[n])
+        c = zat(ORDER[n])
         for copy in passes[n]:
             copy.wait_recv()
         for j in range(2):
@@ -170,12 +175,15 @@
     mean_sent = {}
 
     def total(n):
-        t = IN_ORDER[n]
-        c = zat(t)
+        c = zat(ORDER[n])
         for copy in finals[n]:
             copy.wait_recv()
         for j in range(NX):
             mean[c, j] = summed[y, c * NX + j] + fin_up[c, j] + fin_dn[c, j]
+
+    def scatter(n):
+        t = ORDER[n]
+        c = zat(t)
         for dx in range(NX):
             if (t, dx) == (0, 0):
                 meant[z, x] = mean[z, x]
@@ -200,7 +208,9 @@
         q_x[t, 2] = send(here, here, qx_s.at[t, 2], qx_r.at[t, 2], peer(0, dx))
 
     def project(n):
-        c = zat(IN_ORDER[n])
+        t = ORDER[n]
+        c = zat(t)
+        q_x[(NZ - t) % NZ, 2].wait_recv()
         part = dot(mean[c, 0], q_all[c, 0], NT)
         for j in range(1, NX):
             part = part + dot(mean[c, j], q_all[c, j], NT)
@@ -209,31 +219,25 @@
         else:
             acc[...] += part
 
-    steps = len(IN_ORDER)
-    for n in range(steps):
-        merge(n)
+    steps = len(ORDER)
+    merge(0)
+    pl.semaphore_wait(barrier, len(near))
+    swap_cores(0)
     q_load.wait()
-    pl.semaphore_wait(barrier, 3 + len(PEERS))
-
-    for n in range(steps):
-        swap_cores(n)
-    spread_q(0)
     plan = [
-        (pair_sum, 0), (pair_sum, 1), (pair_sum, 2), (pair_sum, 3), (spread_q, 1), (spread_q, 7),
-        (pair_sum, 4), (pair_sum, 5), (pair_sum, 6), (pair_sum, 7), (relay_q, 0), (pass_on, 0), (pass_on, 1),
-        (spread_q, 2), (spread_q, 6), (relay_q, 1), (relay_q, 7), (pass_on, 2), (pass_on, 3), (total, 0),
-        (spread_q, 3), (spread_q, 5), (relay_q, 2), (relay_q, 6), (pass_on, 4), (total, 1), (pass_on, 5),
-        (total, 2), (spread_q, 4), (relay_q, 3), (relay_q, 5), (pass_on, 6), (total, 3), (pass_on, 7),
-        (total, 4), (relay_q, 4), (total, 5), (total, 6),
+        (merge, 1), (swap_cores, 1), (spread_q, 0), (merge, 2), (swap_cores, 2), (pair_sum, 0), (merge, 3),
+        (swap_cores, 3), (pair_sum, 1), (merge, 4), (swap_cores, 4), (pair_sum, 2), (merge, 5), (swap_cores, 5),
+        (pair_sum, 3), (merge, 6), (swap_cores, 6), (pair_sum, 4), (merge, 7), (swap_cores, 7), (pair_sum, 5),
+        (pair_sum, 6), (pair_sum, 7), (pass_on, 0), (spread_q, 1), (spread_q, 7), (pass_on, 1), (pass_on, 2),
+        (relay_q, 0), (pass_on, 3), (spread_q, 2), (spread_q, 6), (pass_on, 4), (relay_q, 1), (relay_q, 7),
+        (pass_on, 5), (pass_on, 6), (pass_on, 7), (total, 0), (project, 0), (scatter, 0), (spread_q, 3),
+        (spread_q, 5), (total, 1), (project, 1), (scatter, 1), (relay_q, 2), (relay_q, 6), (total, 2),
+        (project, 2), (scatter, 2), (spread_q, 4), (total, 3), (project, 3), (scatter, 3), (relay_q, 3),
+        (relay_q, 5), (total, 4), (project, 4), (scatter, 4), (relay_q, 4), (total, 5), (project, 5), (scatter, 5),
+        (total, 6), (project, 6), (scatter, 6), (total, 7), (project, 7),
     ]
     for step, n in plan:
         step(n)
-    for t in range(NZ):
-        q_x[t, 2].wait_recv()
-    for n in range(steps - 1):
-        project(n)
-    total(steps - 1)
-    project(steps - 1)
 
     half_out[0] = acc[:16]
     half_out[1] = acc[16:]
@@ -242,62 +246,64 @@
     mine = (half_out[k] + half_in[...]) * (1.0 / GROUPS)
     left[z, x, k] = jnp.concatenate([mine[:8], mine[8:]], axis=1)
     spread = [
-        send(left.at[z, x, k], left.at[z, x, k], l_s.at[t, dx], l_r.at[t, dx], peer(t, dx)) for t, dx in PEERS
+        send(left.at[z, x, k], left.at[z, x, k], l_s.at[t, dx], l_r.at[t, dx], peer(t, dx))
+        for t, dx in reversed(PEERS)
     ]
+    scatter(steps - 1)
+    flush()
     for copy in spread:
         copy.wait_recv()
     cross = send(left.at[:, :, k], left.at[:, :, k], lc_s, lc_r, partner)
     for copy in mean_sent.values():
         copy.wait_recv()
+
+    def rows_of(i, j):
+        return pl.ds(pl.multiple_of(16 * i + 8 * j, 8), 8)
+
+    def products(i):
+        part = left[:, :, i].reshape(NZ * NX * 8, BLOCK)
+        turned = jnp.transpose(part)
+        prod = [dot(turned, meant[:, :, rows_of(i, j)].reshape(NZ * NX * 8, BLOCK)) for j in range(2)]
+        return prod[0][:RANK] + prod[1][RANK:], dot(turned, part)
+
+    proj, square = products(k)
     cross.wait_recv()
-
-    parts = [left[:, :, i].reshape(NZ * NX * 8, BLOCK) for i in range(2)]
-    turned = [jnp.transpose(p) for p in parts]
-    square = dot(turned[0], parts[0]) + dot(turned[1], parts[1])
-    gram = square[:RANK, :RANK] + square[RANK:, RANK:]
-    inv = inverse_factor(gram)
-
-    def rows_of(i, j):
-        return pl.ds(16 * i + 8 * j, 8)
-
-    prod = [
-        sum(dot(turned[i], meant[:, :, rows_of(i, j)].reshape(NZ * NX * 8, BLOCK)) for i in range(2))
-        for j in range(2)
-    ]
-    proj = prod[0][:RANK] + prod[1][RANK:]
-    q_mine = dot(inv, proj) * (1.0 / GROUPS)
-    solved = dot(jnp.transpose(inv), q_mine)
-    v_all[z] = solved
-    v_sent = {}
-    zero = jnp.zeros((RANK, BLOCK), jnp.float32)
+    more = products(other)
+    square = square + more[1]
+    v_all[z] = proj + more[0]
+    v_sent = {t: send(v_all.at[z], v_all.at[z], v_s.at[t], v_r.at[t], peer(t, 0)) for t in (1, 7, 2, 6)}
+    inv = inverse_factor(square[:RANK, :RANK] + square[RANK:, RANK:])
     rows = left[z].reshape(NX * 2 * 8, BLOCK)
-    approx[k, y, 32] = q_mine[:32]
-    approx[k, y, 33] = q_mine[32:]
+    ortho = jnp.concatenate([dot(rows[:, :RANK], inv, NT), dot(rows[:, RANK:], inv, NT)], axis=0)
+    blocks, direct, relay, crossed = {}, {}, {}, {}
+    early = list(sends)
+    sends.clear()
 
     def expand(n):
-        t = OUT_ORDER[n]
+        t = ORDER[n]
         c = (z + NZ - t) % NZ
         if n > 0:
             v_sent[t].wait_recv()
-        ring(lambda c: v_all.at[c], v_s, v_r, v_sent, t)
-        v = v_all[c]
-        for j in range(2):
-            wide = jnp.concatenate([v, zero] if j == 0 else [zero, v], axis=0)
-            got = dot(rows, wide).reshape(NX, 2, 8, BLOCK)
-            for i in range(2):
-                block_out[c, :, rows_of(i, j)] = got[:, i]
+        ring(lambda c: v_all.at[c], v_s, v_r, v_sent, t, ONWARD_FAR)
+        q_part = dot(inv, v_all[c]) * (1.0 / GROUPS)
+        if n == 0:
+            approx[k, y, 32] = q_part[:32]
+            approx[k, y, 33] = q_part[32:]
+        got = dot(ortho, q_part).reshape(2, NX, 2, 8, BLOCK)
+        for i in range(2):
+            for j in range(2):
+                block_out[c, :, rows_of(i, j)] = got[j, :, i]
         for dx in range(1, NX):
             blocks[n, dx] = send(
                 block_out.at[c, xat(dx)], approx.at[k, y, c * NX + x], a_s.at[t, dx], a_r.at[t, dx], peer(0, dx)
             )
         approx[k, y, c * NX + x] = block_out[c, x]
 
-    blocks, direct, relay, crossed = {}, {}, {}, {}
 
     def places(n):
         if n == steps:
             return pl.ds(32, 2), pl.ds(32, 1), pl.ds(33, 1)
-        c = (z + NZ - OUT_ORDER[n]) % NZ
+        c = (z + NZ - ORDER[n]) % NZ
         return four(c), pl.ds(c * NX, 2), pl.ds(c * NX + 2, 2)
 
     def share(n):
@@ -311,6 +317,10 @@
             send(here, here, y_s.at[1, n], y_r.at[1, n], down),
         )
 
+    def cross_over(n, m, slot):
+        here = approx.at[k, m, places(n)[0]]
+        crossed[n, slot] = send(here, here, ac_s.at[slot, n], ac_r.at[slot, n], partner)
+
     def pass_along(n):
         _, first, second = places(n)
         for copy in direct[n]:
@@ -320,21 +330,30 @@
             send(from_dn, from_dn, rel_s.at[0, n], rel_r.at[0, n], up),
             send(from_up, from_up, rel_s.at[1, n], rel_r.at[1, n], down),
         )
+        for slot, m in enumerate((y, y_up, y_dn)):
+            cross_over(n, m, slot)
 
     def over(n):
         for copy in relay[n]:
             copy.wait_recv()
-        here = approx.at[k, :, places(n)[0]]
-        crossed[n] = send(here, here, ac_s.at[n], ac_r.at[n], partner)
+        cross_over(n, y_far, 3)
+
+    def tidy(n):
+        for copy in early:
+            copy.wait_send()
+        early.clear()
+        for _ in range(n):
+            sends.pop(0).wait_send()
 
     def finish(n):
-        crossed[n].wait_recv()
+        for slot in range(MATS):
+            crossed[n, slot].wait_recv()
         if n == steps:
             for m in range(MATS):
                 for h in range(2):
                     q_out[m, :, h * BLOCK : (h + 1) * BLOCK] = approx[h, m, 32:34].reshape(RANK, BLOCK)
             return
-        c = (z + NZ - OUT_ORDER[n]) % NZ
+        c = (z + NZ - ORDER[n]) % NZ
 
         def one(m, _):
             for j in range(2 * NX):
@@ -347,18 +366,16 @@
 
     Q = steps
     plan = [
-        (expand, 0), (share, Q), (share, 0), (expand, 1), (expand, 2), (share, 1), (share, 2), (pass_along, Q),
-        (pass_along, 0), (expand, 3), (expand, 4), (share, 3), (share, 4), (pass_along, 1), (pass_along, 2),
-        (over, Q), (over, 0), (expand, 5), (expand, 6), (share, 5), (share, 6), (pass_along, 3), (pass_along, 4),
-        (over, 1), (over, 2), (expand, 7), (share, 7), (finish, Q), (finish, 0), (pass_along, 5), (pass_along, 6),
-        (over, 3), (over, 4), (finish, 1), (finish, 2), (pass_along, 7), (over, 5), (over, 6), (finish, 3),
-        (finish, 4), (over, 7), (finish, 5), (finish, 6), (finish, 7),
+        (expand, 0), (share, Q), (expand, 1), (expand, 2), (share, 0), (expand, 3), (expand, 4), (share, 1),
+        (share, 2), (pass_along, Q), (pass_along, 0), (expand, 5), (expand, 6), (share, 3), (share, 4),
+        (pass_along, 1), (pass_along, 2), (expand, 7), (over, Q), (over, 0), (share, 5), (share, 6),
+        (pass_along, 3), (pass_along, 4), (over, 1), (over, 2), (share, 7), (finish, Q), (finish, 0),
+        (pass_along, 5), (pass_along, 6), (over, 3), (over, 4), (finish, 1), (finish, 2), (pass_along, 7),
+        (over, 5), (over, 6), (finish, 3), (finish, 4), (tidy, 80), (over, 7), (finish, 5), (finish, 6), (finish, 7),
     ]
     for step, n in plan:
         step(n)
-
-    for copy in sends:
-        copy.wait_send()
+    flush()
 
 
 def body(grads, errors, q_prev):
@@ -406,13 +423,13 @@
             dma((NZ, NX)), dma((NZ, NX)),
             dma((2, 9)), dma((2, 9)),
             dma((2, 9)), dma((2, 9)),
-            dma((9,)), dma((9,)),
+            dma((MATS, 9)), dma((MATS, 9)),
         ],
         name="powersgd",
         compiler_params=pltpu.CompilerParams(
             collective_id=0, has_side_effects=True, vmem_limit_bytes=46 << 20
         ),
-    )(grads, errors, jnp.swapaxes(q_prev, 1, 2))
+    )(*(pltpu.with_memory_space_constraint(v, pltpu.HBM) for v in (grads, errors, jnp.swapaxes(q_prev, 1, 2))))
     return jnp.swapaxes(q_new, 1, 2), errors_new
 
 

time: 92.2 us -> 84.9 us (0.921)
  Pallas kernels: 86.1 us -> 81.4 us
  local copies, waits for them, and re-layouts: 5.25 us -> 2.72 us
    pallas_call x1, Pallas kernels: 86.1 us -> 81.4 us  [body(): pl.pallas_call(kernel, out_shape=(jax.ShapeDtypeStruct((MATS, RANK, 2 * B...]
    unnamed x6 -> x2, local copies, waits for them, and re-layouts: 5.25 us -> 2.72 us
where the time goes in v3:
time: 84.9 us; the launch traced here: 84.8 us
  Pallas kernels  81.4 us (96%)
  local copies, waits for them, and re-layouts  2.72 us (3%)
    pallas_call x1, Pallas kernels, body(): pl.pallas_call(kernel, out_shape=(jax.ShapeDtypeStruct((MATS, RANK, 2 * B...  81.4 us
    unnamed x2, local copies, waits for them, and re-layouts  2.72 us

profile of v3, /device:TPU:1, one launch (start us, length us, event | category | flops | bytes accessed | tf_op | source)
XLA Modules:
  0.0 84.8 jit_solution(17278555798742171565)
XLA Ops:
  0.6 81.4 %powersgd.1 = (f32[4,64,256]{2,1,0:T(8,128)S(1)}, f32[1,4,32,8192]{3,2,1,0:T(8,128)S(1)}) custom-call(bf16[1,4,32,8192]{3,2,1,0:T(8,128)(2,1)} %grads.1, f32[1,4,32,8192]{3,2,1,0:T(8,128)} %errors.1, f32[4,64,256]{2,1,0:T(8,128)} %bitcast.3), custom_call_target="tpu_custom_call" | custom-call | tf_op jit(solution)/shard_map/powersgd/pallas_call | solution.py:385
  82.1 0.7 copy.7
  82.8 2.0 %copy.8 = f32[1,4,32,8192]{3,2,1,0:T(8,128)} copy(f32[1,4,32,8192]{3,2,1,0:T(8,128)S(1)} %get-tuple-element.9) | data formatting | bytes 8388608

commit v4 on v3

--- a/solution.py
+++ b/solution.py
@@ -17,6 +17,7 @@
 NT = (((1,), (1,)), ((), ()))
 
 ORDER = (0, 1, 7, 2, 6, 3, 5, 4)
+IN_ORDER = (4, 3, 5, 2, 6, 1, 7, 0)
 ONWARD = {0: (1, 7), 1: (2,), 2: (3,), 3: (4,), 4: (), 5: (), 6: (5,), 7: (6,)}
 ONWARD_FAR = {2: (3,), 3: (4,), 6: (5,)}
 PEERS = tuple((t, dx) for t in ORDER for dx in range(NX) if (t, dx) != (0, 0))
@@ -65,7 +66,7 @@
     grads, errors, q_prev, q_out, e_out,
     g_in, e_in, merged, summed, pass_up, pass_dn, fin_up, fin_dn, mean, meant, q_all,
     acc, half_out, half_in, left, v_all, block_out, approx,
-    ld_sem, q_sem, core_s, core_r, pass_s, pass_r, fin_s, fin_r, m_s, m_r, qz_s, qz_r, qx_s, qx_r,
+    ld_sem, q_sem, core_s, core_r, pass_s, pass_r, fin_s, fin_r, m_s, m_r, qz_s, qz_r, qx_s, qx_r, x_known, z_known,
     h_s, h_r, v_s, v_r, l_s, l_r, lc_s, lc_r, a_s, a_r, y_s, y_r, rel_s, rel_r, ac_s, ac_r,
 ):
     d, r = lax.axis_index("dp"), lax.axis_index("rows")
@@ -110,7 +111,7 @@
         q_prev.at[y, :, pl.ds(pl.multiple_of(k * BLOCK, BLOCK), BLOCK)], q_all.at[z, x], q_sem
     )
     q_load.start()
-    for n, t in enumerate(ORDER):
+    for n, t in enumerate(IN_ORDER):
         at = pl.ds(pl.multiple_of(zat(t) * CHUNK, CHUNK), CHUNK)
         loads[n] = (
             pltpu.make_async_copy(grads.at[0, :, :, at], g_in.at[zat(t)], ld_sem.at[0, n]),
@@ -129,7 +130,7 @@
         return pl.ds(pl.multiple_of(c * NX, NX), NX)
 
     def merge(n):
-        c = zat(ORDER[n])
+        c = zat(IN_ORDER[n])
         for load in loads[n]:
             load.wait()
 
@@ -142,11 +143,11 @@
         lax.fori_loop(0, MATS, one, 0)
 
     def swap_cores(n):
-        c = zat(ORDER[n])
+        c = zat(IN_ORDER[n])
         core[n] = send(merged.at[:, other, four(c)], summed.at[:, four(c)], core_s.at[n], core_r.at[n], partner)
 
     def pair_sum(n):
-        c = zat(ORDER[n])
+        c = zat(IN_ORDER[n])
         core[n].wait_recv()
 
         def one(m, _):
@@ -161,7 +162,7 @@
         )
 
     def pass_on(n):
-        c = zat(ORDER[n])
+        c = zat(IN_ORDER[n])
         for copy in passes[n]:
             copy.wait_recv()
         for j in range(2):
@@ -175,14 +176,14 @@
     mean_sent = {}
 
     def total(n):
-        c = zat(ORDER[n])
+        c = zat(IN_ORDER[n])
         for copy in finals[n]:
             copy.wait_recv()
         for j in range(NX):
             mean[c, j] = summed[y, c * NX + j] + fin_up[c, j] + fin_dn[c, j]
 
     def scatter(n):
-        t = ORDER[n]
+        t = IN_ORDER[n]
         c = zat(t)
         for dx in range(NX):
             if (t, dx) == (0, 0):
@@ -192,6 +193,21 @@
                     mean.at[c, xat(dx)], meant.at[z, x], m_s.at[t, dx], m_r.at[t, dx], peer(t, dx)
                 )
 
+    def hello(n):
+        if n == 1:
+            pl.semaphore_wait(x_known, 1)
+        elif n == 5:
+            pl.semaphore_wait(z_known.at[0, 3], 1)
+        elif n > 1:
+            for way in range(2):
+                pl.semaphore_wait(z_known.at[way, n - 2], 1)
+        if n == 0:
+            pl.semaphore_signal(x_known, inc=1, device_id=peer(0, 1), device_id_type=MESH)
+        elif n < 5:
+            for way in range(2 if n < 4 else 1):
+                to = peer((1, 7)[way], 0)
+                pl.semaphore_signal(z_known.at[way, n - 1], inc=1, device_id=to, device_id_type=MESH)
+
     def spread_q(t):
         if t > 0:
             q_z[t].wait_recv()
@@ -208,33 +224,32 @@
         q_x[t, 2] = send(here, here, qx_s.at[t, 2], qx_r.at[t, 2], peer(0, dx))
 
     def project(n):
-        t = ORDER[n]
+        t = IN_ORDER[n]
         c = zat(t)
         q_x[(NZ - t) % NZ, 2].wait_recv()
         part = dot(mean[c, 0], q_all[c, 0], NT)
         for j in range(1, NX):
             part = part + dot(mean[c, j], q_all[c, j], NT)
-        if n == 0:
-            acc[...] = part
-        else:
-            acc[...] += part
-
-    steps = len(ORDER)
+        acc[...] += part
+
+    steps = len(IN_ORDER)
     merge(0)
     pl.semaphore_wait(barrier, len(near))
     swap_cores(0)
     q_load.wait()
+    acc[...] = jnp.zeros_like(acc)
     plan = [
-        (merge, 1), (swap_cores, 1), (spread_q, 0), (merge, 2), (swap_cores, 2), (pair_sum, 0), (merge, 3),
-        (swap_cores, 3), (pair_sum, 1), (merge, 4), (swap_cores, 4), (pair_sum, 2), (merge, 5), (swap_cores, 5),
-        (pair_sum, 3), (merge, 6), (swap_cores, 6), (pair_sum, 4), (merge, 7), (swap_cores, 7), (pair_sum, 5),
-        (pair_sum, 6), (pair_sum, 7), (pass_on, 0), (spread_q, 1), (spread_q, 7), (pass_on, 1), (pass_on, 2),
-        (relay_q, 0), (pass_on, 3), (spread_q, 2), (spread_q, 6), (pass_on, 4), (relay_q, 1), (relay_q, 7),
-        (pass_on, 5), (pass_on, 6), (pass_on, 7), (total, 0), (project, 0), (scatter, 0), (spread_q, 3),
-        (spread_q, 5), (total, 1), (project, 1), (scatter, 1), (relay_q, 2), (relay_q, 6), (total, 2),
-        (project, 2), (scatter, 2), (spread_q, 4), (total, 3), (project, 3), (scatter, 3), (relay_q, 3),
-        (relay_q, 5), (total, 4), (project, 4), (scatter, 4), (relay_q, 4), (total, 5), (project, 5), (scatter, 5),
-        (total, 6), (project, 6), (scatter, 6), (total, 7), (project, 7),
+        (hello, 0), (merge, 1), (swap_cores, 1), (spread_q, 0), (merge, 2), (swap_cores, 2), (pair_sum, 0),
+        (hello, 1), (merge, 3), (swap_cores, 3), (pair_sum, 1), (merge, 4), (swap_cores, 4), (pair_sum, 2),
+        (merge, 5), (swap_cores, 5), (hello, 2), (pair_sum, 3), (merge, 6), (swap_cores, 6), (pair_sum, 4),
+        (merge, 7), (swap_cores, 7), (pair_sum, 5), (hello, 3), (pair_sum, 6), (pair_sum, 7), (pass_on, 0),
+        (spread_q, 1), (spread_q, 7), (pass_on, 1), (hello, 4), (pass_on, 2), (relay_q, 0), (pass_on, 3),
+        (spread_q, 2), (spread_q, 6), (pass_on, 4), (relay_q, 1), (relay_q, 7), (hello, 5), (pass_on, 5),
+        (pass_on, 6), (pass_on, 7), (total, 0), (scatter, 0), (spread_q, 3), (spread_q, 5), (total, 1),
+        (scatter, 1), (relay_q, 2), (relay_q, 6), (total, 2), (scatter, 2), (spread_q, 4), (total, 3),
+        (scatter, 3), (relay_q, 3), (relay_q, 5), (total, 4), (scatter, 4), (project, 4), (project, 3),
+        (relay_q, 4), (total, 5), (scatter, 5), (project, 5), (project, 1), (project, 2), (total, 6),
+        (scatter, 6), (project, 6), (project, 0), (total, 7), (scatter, 7), (project, 7),
     ]
     for step, n in plan:
         step(n)
@@ -249,7 +264,6 @@
         send(left.at[z, x, k], left.at[z, x, k], l_s.at[t, dx], l_r.at[t, dx], peer(t, dx))
         for t, dx in reversed(PEERS)
     ]
-    scatter(steps - 1)
     flush()
     for copy in spread:
         copy.wait_recv()
@@ -376,6 +390,15 @@
     for step, n in plan:
         step(n)
     flush()
+
+
+def store(e_in, q_in, e_out, q_out, sem):
+    copies = [pltpu.make_async_copy(e_in.at[:, m], e_out.at[:, m], sem.at[m]) for m in range(MATS)]
+    copies.append(pltpu.make_async_copy(q_in, q_out, sem.at[MATS]))
+    for copy in copies:
+        copy.start()
+    for copy in copies:
+        copy.wait()
 
 
 def body(grads, errors, q_prev):
@@ -416,6 +439,7 @@
             dma((NZ, NX)), dma((NZ, NX)),
             dma((NZ,)), dma((NZ,)),
             dma((NZ, NX)), dma((NZ, NX)),
+            pltpu.SemaphoreType.REGULAR, pltpu.SemaphoreType.REGULAR((2, 4)),
             dma, dma,
             dma((NZ,)), dma((NZ,)),
             dma((NZ, NX)), dma((NZ, NX)),
@@ -430,6 +454,15 @@
             collective_id=0, has_side_effects=True, vmem_limit_bytes=46 << 20
         ),
     )(*(pltpu.with_memory_space_constraint(v, pltpu.HBM) for v in (grads, errors, jnp.swapaxes(q_prev, 1, 2))))
+    errors_new, q_new = pl.pallas_call(
+        store,
+        out_shape=(jax.ShapeDtypeStruct(errors_new.shape, f32), jax.ShapeDtypeStruct(q_new.shape, f32)),
+        in_specs=[pl.BlockSpec(memory_space=pltpu.VMEM)] * 2,
+        out_specs=(pl.BlockSpec(memory_space=pl.ANY),) * 2,
+        scratch_shapes=[dma((MATS + 1,))],
+        name="store",
+        compiler_params=pltpu.CompilerParams(vmem_limit_bytes=16 << 20),
+    )(*(pltpu.with_memory_space_constraint(v, pltpu.VMEM) for v in (errors_new, q_new)))
     return jnp.swapaxes(q_new, 1, 2), errors_new
 
 

time: 84.9 us -> 82.9 us (0.976)
  local copies, waits for them, and re-layouts: 2.72 us -> 0 us
    unnamed x2 -> x0, local copies, waits for them, and re-layouts: 2.72 us -> none
    pallas_call x0 -> x1, Pallas kernels: none -> 2.13 us  [body(): pl.pallas_call(store, out_shape=(jax.ShapeDtypeStruct(errors_new.shape, f...]
    pallas_call x1, Pallas kernels: 81.4 us -> 80 us  [body(): pl.pallas_call(kernel, out_shape=(jax.ShapeDtypeStruct((MATS, RANK, 2 * B...]
where the time goes in v4:
time: 82.9 us; the launch traced here: 82.8 us
  Pallas kernels  82.1 us (99%)
    pallas_call x1, Pallas kernels, body(): pl.pallas_call(kernel, out_shape=(jax.ShapeDtypeStruct((MATS, RANK, 2 * B...  80 us
    pallas_call x1, Pallas kernels, body(): pl.pallas_call(store, out_shape=(jax.ShapeDtypeStruct(errors_new.shape, f...  2.13 us

profile of v4, /device:TPU:1, one launch (start us, length us, event | category | flops | bytes accessed | tf_op | source)
XLA Modules:
  0.0 82.8 jit_solution(1220136581546995874)
XLA Ops:
  0.6 80.0 %powersgd.1 = (f32[4,64,256]{2,1,0:T(8,128)S(1)}, f32[1,4,32,8192]{3,2,1,0:T(8,128)S(1)}) custom-call(bf16[1,4,32,8192]{3,2,1,0:T(8,128)(2,1)} %grads.1, f32[1,4,32,8192]{3,2,1,0:T(8,128)} %errors.1, f32[4,64,256]{2,1,0:T(8,128)} %bitcast.2), custom_call_target="tpu_custom_call" | custom-call | tf_op jit(solution)/shard_map/powersgd/pallas_call | solution.py:408
  80.6 2.1 %store.1 = (f32[1,4,32,8192]{3,2,1,0:T(8,128)}, f32[4,64,256]{2,1,0:T(8,128)}) custom-call(f32[1,4,32,8192]{3,2,1,0:T(8,128)S(1)} %get-tuple-element.6.e_in, f32[4,64,256]{2,1,0:T(8,128)S(1)} %get-tuple-element.7.q_in), custom_call_target="tpu_custom_call" | custom-call | tf_op jit(solution)/shard_map/store/pallas_call | solution.py:457

commit v5 on v4

--- a/solution.py
+++ b/solution.py
@@ -268,23 +268,26 @@
     for copy in spread:
         copy.wait_recv()
     cross = send(left.at[:, :, k], left.at[:, :, k], lc_s, lc_r, partner)
+
+    def rows_of(i, j):
+        return pl.ds(pl.multiple_of(16 * i + 8 * j, 8), 8)
+
+    def gram_of(i):
+        part = left[:, :, i].reshape(NZ * NX * 8, BLOCK)
+        turned = jnp.transpose(part)
+        return turned, dot(turned, part)
+
+    def projection(i, turned):
+        prod = [dot(turned, meant[:, :, rows_of(i, j)].reshape(NZ * NX * 8, BLOCK)) for j in range(2)]
+        return prod[0][:RANK] + prod[1][RANK:]
+
+    turned, square = gram_of(k)
+    cross.wait_recv()
+    turned_other, more = gram_of(other)
+    square = square + more
     for copy in mean_sent.values():
         copy.wait_recv()
-
-    def rows_of(i, j):
-        return pl.ds(pl.multiple_of(16 * i + 8 * j, 8), 8)
-
-    def products(i):
-        part = left[:, :, i].reshape(NZ * NX * 8, BLOCK)
-        turned = jnp.transpose(part)
-        prod = [dot(turned, meant[:, :, rows_of(i, j)].reshape(NZ * NX * 8, BLOCK)) for j in range(2)]
-        return prod[0][:RANK] + prod[1][RANK:], dot(turned, part)
-
-    proj, square = products(k)
-    cross.wait_recv()
-    more = products(other)
-    square = square + more[1]
-    v_all[z] = proj + more[0]
+    v_all[z] = projection(k, turned) + projection(other, turned_other)
     v_sent = {t: send(v_all.at[z], v_all.at[z], v_s.at[t], v_r.at[t], peer(t, 0)) for t in (1, 7, 2, 6)}
     inv = inverse_factor(square[:RANK, :RANK] + square[RANK:, RANK:])
     rows = left[z].reshape(NX * 2 * 8, BLOCK)

time: 82.9 us -> 82.9 us (level)
  no operation moved by 1% of the time
where the time goes in v5:
time: 82.9 us; the launch traced here: 82.8 us
  Pallas kernels  82.2 us (99%)
    pallas_call x1, Pallas kernels, body(): pl.pallas_call(kernel, out_shape=(jax.ShapeDtypeStruct((MATS, RANK, 2 * B...  80 us
    pallas_call x1, Pallas kernels, body(): pl.pallas_call(store, out_shape=(jax.ShapeDtypeStruct(errors_new.shape, f...  2.13 us

profile of v5, /device:TPU:1, one launch (start us, length us, event | category | flops | bytes accessed | tf_op | source)
XLA Modules:
  0.0 82.8 jit_solution(1773797868473992198)
XLA Ops:
  0.6 80.0 %powersgd.1 = (f32[4,64,256]{2,1,0:T(8,128)S(1)}, f32[1,4,32,8192]{3,2,1,0:T(8,128)S(1)}) custom-call(bf16[1,4,32,8192]{3,2,1,0:T(8,128)(2,1)} %grads.1, f32[1,4,32,8192]{3,2,1,0:T(8,128)} %errors.1, f32[4,64,256]{2,1,0:T(8,128)} %bitcast.2), custom_call_target="tpu_custom_call" | custom-call | tf_op jit(solution)/shard_map/powersgd/pallas_call | solution.py:411
  80.7 2.1 %store.1 = (f32[1,4,32,8192]{3,2,1,0:T(8,128)}, f32[4,64,256]{2,1,0:T(8,128)}) custom-call(f32[1,4,32,8192]{3,2,1,0:T(8,128)S(1)} %get-tuple-element.6.e_in, f32[4,64,256]{2,1,0:T(8,128)S(1)} %get-tuple-element.7.q_in), custom_call_target="tpu_custom_call" | custom-call | tf_op jit(solution)/shard_map/store/pallas_call | solution.py:460
